TPU v7x, 32 devices: a whole 2x2x4 slice. The times are simulated.
32 devices in a mesh: groups: 2 (over y), tok: 4 (over x, core), blk: 4 (over z).
Axes of the slice: x: 2, y: 2, z: 4, core: 2. Of those that a mesh axis runs over, the one named last changes fastest.
Arguments:
- activations: bfloat16 [2048, 6144], P(('groups', 'tok')), parts along dimension 0, may hold values from -6 to 6
- directions: float32 [12288, 256], P(('groups', 'tok'), 'blk'), parts along dimension 0, may hold values from -6 to 6
- block_rank: int32 [4], replicated, may hold values from 0 to 3, each once
Outputs:
- updated: float32 [12288, 256], P(('groups', 'tok'), 'blk'), parts along dimension 0
There are 2 independent parts, one for each index of `groups`. A program takes and returns all parts, laid end to end along the dimension named above; an argument that names none is the same for every part. Nothing has to cross between parts.
Inputs may be any that keep to these rules, and one draw needn't show every extreme that they name: `block_rank`: a permutation of the block numbers.
All inputs are finite; a program needn't handle non-finite values.
Results may differ from a plain program's by a relative error of at most 0.006.
Values may be sent and summed in bfloat16 or wider, within the bound.
A program may use at most 64 MiB of HBM per device.

v0:
```python
import jax
import jax.numpy as jnp
from jax import lax
from jax.sharding import PartitionSpec as P

BW = 64
ITERS = 3


def block_ranks(block_rank, index):
    blocks = index // BW
    table = (blocks[:, None] == jnp.arange(block_rank.shape[0], dtype=jnp.int32)[None, :]).astype(
        jnp.int32
    )
    return (blocks, jnp.sum(table * block_rank[None, :], axis=1))


def split_parts(weighted):
    high = lax.optimization_barrier(weighted.astype(jnp.bfloat16))
    rest = (weighted - high.astype(jnp.float32)).astype(jnp.bfloat16)
    return (high, rest)


def body(activations, directions, block_rank):
    width = activations.shape[1]
    total_tokens = activations.shape[0] * lax.axis_size("tok")
    count = BW * lax.axis_size("blk")
    mine = lax.axis_index("blk")
    own_index = mine * BW + jnp.arange(BW, dtype=jnp.int32)
    all_index = jnp.arange(count, dtype=jnp.int32)
    own_blocks, own_ranks = block_ranks(block_rank, own_index)
    all_blocks, all_ranks = block_ranks(block_rank, all_index)
    contract = (((1,), (1,)), ((), ()))
    features = lax.all_to_all(activations, "tok", split_axis=1, concat_axis=0, tiled=True)
    current = directions
    for step in range(ITERS):
        low = current.astype(jnp.bfloat16)
        proj = jnp.dot(
            activations,
            lax.all_gather(low, "tok", axis=0, tiled=True),
            preferred_element_type=jnp.float32,
        ).astype(jnp.bfloat16)
        cov_dir = (
            lax.dot_general(
                features,
                lax.all_gather(proj, "tok", axis=0, tiled=True),
                (((0,), (0,)), ((), ())),
                preferred_element_type=jnp.float32,
            )
            / total_tokens
        )
        partial_rows = lax.dot_general(
            proj,
            lax.all_gather(proj, "blk", axis=1, tiled=True),
            (((0,), (0,)), ((), ())),
            preferred_element_type=jnp.float32,
        )
        cross_row = lax.psum(partial_rows, "tok") / (total_tokens * width)
        before = all_ranks[None, :] < own_ranks[:, None]
        inside = (all_blocks[None, :] == own_blocks[:, None]) & (
            all_index[None, :] < own_index[:, None]
        )
        high, rest = split_parts((before | inside).astype(jnp.float32) * cross_row)
        piece = lax.all_gather(low, "blk", axis=1, tiled=True)
        total = lax.dot_general(piece, high, contract, preferred_element_type=jnp.float32)
        penalty = total + lax.dot_general(piece, rest, contract, preferred_element_type=jnp.float32)
        moved = current + 0.5 * (cov_dir - penalty)
        squares = lax.psum(jnp.sum(moved * moved, axis=0), "tok")
        scale = jnp.sqrt(squares / width + 1e-06)
        current = moved / scale[None, :]
    return current


def solution(mesh):
    placed = (P(("groups", "tok"), None), P(("groups", "tok"), "blk"), P())
    return jax.shard_map(
        body, mesh=mesh, in_specs=placed, out_specs=P(("groups", "tok"), "blk"), check_vma=False
    )
```

profile of v0, /device:TPU:0, one launch (start us, length us, event | category | flops | bytes accessed | tf_op | source)
XLA Modules:
  0.0 275.9 jit_solution(11110110296924265216)
XLA Ops:
  6.5 4.7 %copy.6 = bf16[256,6144]{0,1:T(8,128)(2,1)} copy(bf16[256,6144]{1,0:T(8,128)(2,1)} %param.3) | data formatting | bytes 6291456 | tf_op args[0]
  11.2 4.9 %all-to-all-start = ((bf16[256,4,1536]{0,2,1:T(8,128)(2,1)}), bf16[256,4,1536]{0,2,1:T(8,128)(2,1)}, u32[]{:S(2)}, u32[]{:S(2)}) async-start(bf16[256,4,1536]{0,2,1:T(8,128)(2,1)} %bitcast.43), calls=%async_computation | async-start | bytes 6291456 | tf_op jit(solution)/shard_map/all_to_all | solution.py:34
  17.2 41.5 %all_gather.36 = bf16[6144,64]{0,1:T(8,128)(2,1)S(1)} all-gather(bf16[1536,64]{0,1:T(8,128)(2,1)S(1)} %convert_element_type.56), channel_id=1, replica_groups=mesh['groups'=2,'tok'=4,'blk'=4] {'tok'}, dimensions={0}, use_global_device_ids=true | all-gather | bytes 983040 | tf_op jit(solution)/shard_map/all_gather | solution.py:40
  59.8 14.4 %all_gather.38 = bf16[256,256]{0,1:T(8,128)(2,1)S(1)} all-gather(bf16[256,64]{0,1:T(8,128)(2,1)S(1)} %convolution_convert_fusion.2), channel_id=1, replica_groups=mesh['groups'=2,'tok'=4,'blk'=4] {'blk'}, dimensions={1}, use_global_device_ids=true | all-gather | bytes 163840 | tf_op jit(solution)/shard_map/all_gather | solution.py:54
  75.3 18.1 %all_gather.39 = bf16[1536,256]{0,1:T(8,128)(2,1)S(1)} all-gather(bf16[1536,64]{0,1:T(8,128)(2,1)S(1)} %convert_element_type.56), channel_id=1, replica_groups=mesh['groups'=2,'tok'=4,'blk'=4] {'blk'}, dimensions={1}, use_global_device_ids=true | all-gather | bytes 983040 | tf_op jit(solution)/shard_map/all_gather | solution.py:64
  93.4 5.9 %all_gather.37 = bf16[1024,64]{0,1:T(8,128)(2,1)} all-gather(bf16[256,64]{0,1:T(8,128)(2,1)S(1)} %convolution_convert_fusion.2), channel_id=1, replica_groups=mesh['groups'=2,'tok'=4,'blk'=4] {'tok'}, dimensions={0}, use_global_device_ids=true | all-gather | bytes 163840 | tf_op jit(solution)/shard_map/all_gather | solution.py:46
  99.3 7.2 %all-reduce.4.cloned.1.call-done = f32[64,256]{1,0:T(8,128)} async-done(((f32[64,256]{1,0:T(8,128)}), f32[64,256]{1,0:T(8,128)}) %all-reduce.4.cloned.1.call-update) | async-done | bytes 65552 | tf_op jit(solution)/shard_map/psum | solution.py:58
  109.6 3.2 %copy.7 = bf16[4,256,1536]{2,1,0:T(8,128)(2,1)S(1)} copy(bf16[4,256,1536]{1,2,0:T(8,128)(2,1)} %bitcast.1) | data formatting | bytes 6291456 | tf_op jit(solution)/shard_map/all_to_all | solution.py:34
  112.9 3.1 %multiply_reduce_fusion.2 = (f32[64]{0:T(128)}, f32[1536,64]{0,1:T(8,128)}) fusion(f32[1536,64]{0,1:T(8,128)S(1)} %copy-done.1, f32[64,1536]{1,0:T(8,128)} %convolution_add_fusion.2, bf16[1024,64]{0,1:T(8,128)(2,1)} %all_gather.37, bf16[1024,1536]{1,0:T(8,128)(2,1)S(1)} %bitcast.40), kind=kOutput, calls=%fused_computation.23 | convolution fusion | flops 201916352 | bytes 4456704 | tf_op jit(solution)/shard_map/dot_general | solution.py:44
  116.0 5.9 %psum.43 = f32[64]{0:T(128)S(1)} all-reduce(f32[64]{0:T(128)} %get-tuple-element.5), channel_id=1, replica_groups=mesh['groups'=2,'tok'=4,'blk'=4] {'tok'}, use_global_device_ids=true, to_apply=%region_4.5 | all-reduce | flops 64 | bytes 512 | tf_op jit(solution)/shard_map/psum | solution.py:68
  122.9 8.1 %all_gather.40 = bf16[6144,64]{0,1:T(8,128)(2,1)S(1)} all-gather(bf16[1536,64]{0,1:T(8,128)(2,1)S(1)} %fusion.12), channel_id=1, replica_groups=mesh['groups'=2,'tok'=4,'blk'=4] {'tok'}, dimensions={0}, use_global_device_ids=true | all-gather | bytes 983040 | tf_op jit(solution)/shard_map/all_gather | solution.py:40
  131.1 3.0 %convolution_convert_fusion.1 = bf16[64,256]{1,0:T(8,128)(2,1)S(1)} fusion(bf16[6144,64]{0,1:T(8,128)(2,1)S(1)} %all_gather.40, bf16[256,6144]{1,0:T(8,128)(2,1)} %param.3), kind=kOutput, calls=%fused_computation.19 | convolution fusion | flops 201342976 | bytes 3964928 | tf_op jit(solution)/shard_map/dot_general | solution.py:38
  134.0 13.5 %all_gather.43 = bf16[256,256]{0,1:T(8,128)(2,1)S(1)} all-gather(bf16[256,64]{0,1:T(8,128)(2,1)S(1)} %bitcast.44), channel_id=1, replica_groups=mesh['groups'=2,'tok'=4,'blk'=4] {'blk'}, dimensions={1}, use_global_device_ids=true | all-gather | bytes 163840 | tf_op jit(solution)/shard_map/all_gather | solution.py:54
  147.5 5.4 %all_gather.41 = bf16[1024,64]{0,1:T(8,128)(2,1)S(1)} all-gather(bf16[256,64]{0,1:T(8,128)(2,1)S(1)} %bitcast.45), channel_id=1, replica_groups=mesh['groups'=2,'tok'=4,'blk'=4] {'tok'}, dimensions={0}, use_global_device_ids=true | all-gather | bytes 163840 | tf_op jit(solution)/shard_map/all_gather | solution.py:46
  155.2 20.0 %all_gather.42 = bf16[1536,256]{0,1:T(8,128)(2,1)} all-gather(bf16[1536,64]{0,1:T(8,128)(2,1)S(1)} %fusion.12), channel_id=1, replica_groups=mesh['groups'=2,'tok'=4,'blk'=4] {'blk'}, dimensions={1}, use_global_device_ids=true | all-gather | bytes 983040 | tf_op jit(solution)/shard_map/all_gather | solution.py:64
  175.1 10.4 %all-reduce.6.cloned.1.call-done = f32[64,256]{1,0:T(8,128)} async-done(((f32[64,256]{1,0:T(8,128)}), f32[64,256]{1,0:T(8,128)}) %all-reduce.6.cloned.1.call-update) | async-done | bytes 65552 | tf_op jit(solution)/shard_map/psum | solution.py:58
  190.4 5.8 %psum.45 = f32[64]{0:T(128)S(1)} all-reduce(f32[64]{0:T(128)S(1)} %get-tuple-element.7), channel_id=1, replica_groups=mesh['groups'=2,'tok'=4,'blk'=4] {'tok'}, use_global_device_ids=true, to_apply=%region_7.8 | all-reduce | flops 64 | bytes 512 | tf_op jit(solution)/shard_map/psum | solution.py:68
  197.3 8.1 %all_gather.44 = bf16[6144,64]{0,1:T(8,128)(2,1)S(1)} all-gather(bf16[1536,64]{0,1:T(8,128)(2,1)S(1)} %fusion.13), channel_id=1, replica_groups=mesh['groups'=2,'tok'=4,'blk'=4] {'tok'}, dimensions={0}, use_global_device_ids=true | all-gather | bytes 983040 | tf_op jit(solution)/shard_map/all_gather | solution.py:40
  205.4 3.0 %convolution_convert_fusion = bf16[64,256]{1,0:T(8,128)(2,1)S(1)} fusion(bf16[6144,64]{0,1:T(8,128)(2,1)S(1)} %all_gather.44, bf16[256,6144]{1,0:T(8,128)(2,1)} %param.3), kind=kOutput, calls=%fused_computation.18 | convolution fusion | flops 201342976 | bytes 3964928 | tf_op jit(solution)/shard_map/dot_general | solution.py:38
  208.4 13.5 %all_gather.47 = bf16[256,256]{0,1:T(8,128)(2,1)S(1)} all-gather(bf16[256,64]{0,1:T(8,128)(2,1)S(1)} %bitcast.46), channel_id=1, replica_groups=mesh['groups'=2,'tok'=4,'blk'=4] {'blk'}, dimensions={1}, use_global_device_ids=true | all-gather | bytes 163840 | tf_op jit(solution)/shard_map/all_gather | solution.py:54
  221.9 5.4 %all_gather.45 = bf16[1024,64]{0,1:T(8,128)(2,1)S(1)} all-gather(bf16[256,64]{0,1:T(8,128)(2,1)S(1)} %bitcast.47), channel_id=1, replica_groups=mesh['groups'=2,'tok'=4,'blk'=4] {'tok'}, dimensions={0}, use_global_device_ids=true | all-gather | bytes 163840 | tf_op jit(solution)/shard_map/all_gather | solution.py:46
  229.5 19.6 %all_gather.46 = bf16[1536,256]{0,1:T(8,128)(2,1)S(1)} all-gather(bf16[1536,64]{0,1:T(8,128)(2,1)S(1)} %fusion.13), channel_id=1, replica_groups=mesh['groups'=2,'tok'=4,'blk'=4] {'blk'}, dimensions={1}, use_global_device_ids=true | all-gather | bytes 983040 | tf_op jit(solution)/shard_map/all_gather | solution.py:64
  249.1 10.9 %all-reduce.8.cloned.1.call-done = f32[64,256]{1,0:T(8,128)} async-done(((f32[64,256]{1,0:T(8,128)}), f32[64,256]{1,0:T(8,128)}) %all-reduce.8.cloned.1.call-update) | async-done | bytes 65552 | tf_op jit(solution)/shard_map/psum | solution.py:58
  262.7 5.8 %psum.47 = f32[64]{0:T(128)S(1)} all-reduce(f32[64]{0:T(128)S(1)} %get-tuple-element.9), channel_id=1, replica_groups=mesh['groups'=2,'tok'=4,'blk'=4] {'tok'}, use_global_device_ids=true, to_apply=%region_10.11 | all-reduce | flops 64 | bytes 512 | tf_op jit(solution)/shard_map/psum | solution.py:68
  (44 shorter events, 21.4 us)
Async XLA Ops:
  11.2 47.5 %copy-start = (bf16[256,6144]{1,0:T(8,128)(2,1)S(1)}, bf16[256,6144]{1,0:T(8,128)(2,1)}, u32[]{:S(2)}) copy-start(bf16[256,6144]{1,0:T(8,128)(2,1)} %param.3) | copy-start | bytes 9437188
  11.2 98.4 %all-to-all-start = ((bf16[256,4,1536]{0,2,1:T(8,128)(2,1)}), bf16[256,4,1536]{0,2,1:T(8,128)(2,1)}, u32[]{:S(2)}, u32[]{:S(2)}) async-start(bf16[256,4,1536]{0,2,1:T(8,128)(2,1)} %bitcast.43), calls=%async_computation | async-start | bytes 6291456 | tf_op jit(solution)/shard_map/all_to_all | solution.py:34
  16.1 59.0 %copy-start.4 = (s32[4]{0:T(128)S(1)}, s32[4]{0:T(128)}, u32[]{:S(2)}) copy-start(s32[4]{0:T(128)} %param.5) | copy-start | bytes 52
  16.1 90.4 %all-reduce.4.cloned.1.call-start = ((), (), s32[]{:S(2)}) async-start(), calls=%async_computation.1 | async-start | bytes 131072 | tf_op jit(solution)/shard_map/psum | solution.py:58
  75.1 110.5 %all-reduce.6.cloned.1.call-start = ((), (), s32[]{:S(2)}) async-start(), calls=%async_computation.2 | async-start | bytes 131072 | tf_op jit(solution)/shard_map/psum | solution.py:58
  75.3 34.4 %copy-start.2 = (s32[64]{0:T(128)}, s32[64]{0:T(128)S(1)}, u32[]{:S(2)}) copy-start(s32[64]{0:T(128)S(1)} %select_reduce_fusion.1) | copy-start | bytes 772
  109.6 3.2 %copy-start.1 = (f32[1536,64]{0,1:T(8,128)S(1)}, f32[1536,64]{0,1:T(8,128)}, u32[]{:S(2)}) copy-start(f32[1536,64]{0,1:T(8,128)} %param.4) | copy-start | bytes 1179652
  134.0 51.5 %copy-start.3 = (s32[64]{0:T(128)S(1)}, s32[64]{0:T(128)}, u32[]{:S(2)}) copy-start(s32[64]{0:T(128)} %copy-done.2) | copy-start | bytes 772
  153.7 106.3 %all-reduce.8.cloned.1.call-start = ((), (), s32[]{:S(2)}) async-start(), calls=%async_computation.3 | async-start | bytes 131072 | tf_op jit(solution)/shard_map/psum | solution.py:58
Sparse Core Ops, SparseCore 0:
  75.2 31.2 all-reduce.3
  153.9 31.6 all-reduce.5
  228.2 31.6 all-reduce.7
where the time goes:
time: 277 us; the launch traced here: 276 us
  blocking collectives  191 us (69%)
  waiting for transfers between devices  28.6 us (10%)
  matrix products  23.2 us (8%)
  between operations  13.3 us (5%)
  local copies, waits for them, and re-layouts  7.94 us (3%)
  other arithmetic  7.08 us (3%)
  starting transfers between devices  5.02 us (2%)
    all_gather x3, blocking collectives, body(): lax.all_gather(low, 'tok', axis=0, tiled=True)  57.8 us
    all_gather x3, blocking collectives, body(): piece = lax.all_gather(low, 'blk', axis=1, tiled=True)  57.6 us
    all_gather x3, blocking collectives, body(): lax.all_gather(proj, 'blk', axis=1, tiled=True)  41.3 us
    psum x3, waiting for transfers between devices, body(): cross_row = lax.psum(partial_rows, 'tok') / (total_tokens * width)  28.5 us
    psum x3, blocking collectives, body(): squares = lax.psum(jnp.sum(moved * moved, axis=0), 'tok')  17.4 us
    all_gather x3, blocking collectives, body(): lax.all_gather(proj, 'tok', axis=0, tiled=True)  16.7 us
    dot_general x3, matrix products, body(): jnp.dot(activations, lax.all_gather(low, 'tok', axis=0, tiled=True), pref...  7 us
    dot_general x3, matrix products, body(): lax.dot_general(piece, rest, contract, preferred_element_type=jnp.float32)  5.99 us
  transfers between devices with their start and end apart: 4, of which 3 were waited for; matrix products, arithmetic and copies ran while one was open for 3% of the time, Pallas kernels for 0%

commit v1 on v0

--- a/solution.py
+++ b/solution.py
@@ -1,6 +1,10 @@
+import functools
+
 import jax
 import jax.numpy as jnp
 from jax import lax
+from jax.experimental import pallas as pl
+from jax.experimental.pallas import tpu as pltpu
 from jax.sharding import PartitionSpec as P
 
 BW = 64
@@ -71,8 +75,299 @@
     return current
 
 
+F32, BF16 = jnp.float32, jnp.bfloat16
+MESH = pl.DeviceIdType.MESH
+
+
+def nt(a, b):
+    return lax.dot_general(a, b, (((1,), (1,)), ((), ())), preferred_element_type=F32)
+
+
+def nn(a, b):
+    return jnp.dot(a, b, preferred_element_type=F32)
+
+
+def order_mask(rank_ref, m, count):
+    rows = lax.broadcasted_iota(jnp.int32, (count, count), 0)
+    cols = lax.broadcasted_iota(jnp.int32, (count, count), 1)
+    row_rank = jnp.zeros((count, count), jnp.int32)
+    col_rank = jnp.zeros((count, count), jnp.int32)
+    same = jnp.zeros((count, count), jnp.int32)
+    for k in range(m):
+        in_row = (rows >= k * BW) & (rows < (k + 1) * BW)
+        in_col = (cols >= k * BW) & (cols < (k + 1) * BW)
+        row_rank = jnp.where(in_row, rank_ref[k], row_rank)
+        col_rank = jnp.where(in_col, rank_ref[k], col_rank)
+        same = jnp.where(in_row & in_col, 1, same)
+    inside = (same == 1) & (cols < rows)
+    return jnp.where((col_rank < row_rank) | inside, 1.0, 0.0).astype(F32)
+
+
+def fused(
+    n, m, rank_ref, act_ref, dir_ref, out_ref,
+    feat, low, v32, u32, chain, part, arrived, proj, wsum, half, coef, sq_out, sq_in,
+    f_loc, f_s, f_r, v_s, v_r, p_s, p_r, k_s, k_r, q_s, q_r,
+):
+    i, b = lax.axis_index("tok"), lax.axis_index("blk")
+    tokens, rows = feat.shape[1], feat.shape[2]
+    count = m * BW
+    total_tokens, width = n * tokens, n * rows
+    own = pl.ds(pl.multiple_of(b * BW, BW), BW)
+
+    def ahead(d):
+        return lax.rem(i + d, n)
+
+    def behind(d):
+        return lax.rem(i + n - d, n)
+
+    def blk_ahead(d):
+        return lax.rem(b + d, m)
+
+    def blk_behind(d):
+        return lax.rem(b + m - d, m)
+
+    others = [(d, e) for e in range(m) for d in range(n) if (d, e) != (0, 0)]
+
+    barrier = pltpu.get_barrier_semaphore()
+    for d, e in others:
+        pl.semaphore_signal(
+            barrier, inc=1, device_id={"tok": ahead(d), "blk": blk_ahead(e)}, device_id_type=MESH
+        )
+    pl.semaphore_wait(barrier, len(others))
+
+    sent = []
+
+    def push(src, dst, s, r, d, e):
+        copy = pltpu.make_async_remote_copy(
+            src_ref=src, dst_ref=dst, send_sem=s, recv_sem=r,
+            device_id={"tok": ahead(d), "blk": blk_ahead(e)}, device_id_type=MESH,
+        )
+        copy.start()
+        sent.append(copy)
+
+    def landed(dst, s, r):
+        pltpu.make_async_remote_copy(
+            src_ref=dst, dst_ref=dst, send_sem=s, recv_sem=r,
+            device_id={"tok": ahead(1)}, device_id_type=MESH,
+        ).wait_recv()
+
+    for d in range(1, n):
+        cols = pl.ds(pl.multiple_of(ahead(d) * rows, 128), rows)
+        push(act_ref.at[:, cols], feat.at[i], f_s.at[d], f_r.at[d], d, 0)
+    mine = pltpu.make_async_copy(
+        act_ref.at[:, pl.ds(pl.multiple_of(i * rows, 128), rows)], feat.at[i], f_loc
+    )
+    mine.start()
+    v32[...] = dir_ref[...].T
+    low[own, :] = v32[...].astype(BF16)
+    for e in range(1, m):
+        push(low.at[own], low.at[own], v_s.at[e], v_r.at[e], 0, e)
+    mask = order_mask(rank_ref, m, count)
+    mine.wait()
+
+    def scatter(k, left, first):
+        kept = nt(left, feat[i])
+        for d in range(1, n):
+            j = ahead(d)
+            if first:
+                landed(feat.at[behind(n - d)], f_s.at[n - d], f_r.at[n - d])
+            part[k, d] = nt(left, feat[j])
+            push(part.at[k, d], arrived.at[k, d], p_s.at[k, d], p_r.at[k, d], d, 0)
+        return kept
+
+    def gather(k, kept):
+        for d in range(1, n):
+            landed(arrived.at[k, d], p_s.at[k, d], p_r.at[k, d])
+            kept = kept + arrived[k, d]
+        chain[k, i, own, :] = kept.astype(BF16)
+        for d, e in others:
+            tile = chain.at[k, i, own]
+            push(tile, tile, k_s.at[k, d, e], k_r.at[k, d, e], d, e)
+
+    def chain_landed(k, d, e):
+        peer = pl.ds(pl.multiple_of(blk_behind(e) * BW, BW), BW)
+        landed(chain.at[k, behind(d), peer], k_s.at[k, d, e], k_r.at[k, d, e])
+
+    def to_features(k):
+        total = nn(chain[k, i, own, :], feat[i])
+        for d in range(1, n):
+            chain_landed(k, d, 0)
+            j = behind(d)
+            total = total + nn(chain[k, j, own, :], feat[j])
+        return total * (0.5 / total_tokens)
+
+    def rest_landed(k):
+        for e in range(1, m):
+            for d in range(n):
+                chain_landed(k, d, e)
+
+    def penalised(t, cross):
+        half[t] = mask * cross * (0.5 / (total_tokens * width))
+
+    def send_squares(t, moved, everyone):
+        column = jnp.sum(moved * moved, axis=1, keepdims=True)
+        block = jnp.concatenate(
+            [jnp.broadcast_to(column, (BW, 128)), jnp.zeros((128 - BW, 128), F32)], axis=0
+        )
+        sq_in[t, 0, 0] = block.T[0:8]
+        for d, e in others:
+            if everyone or e == 0:
+                push(sq_in.at[t, 0, 0], sq_in.at[t, d, e], q_s.at[t, d, e], q_r.at[t, d, e], d, e)
+
+    def scale_of(t, e):
+        total = sq_in[t, 0, e]
+        for d in range(1, n):
+            total = total + sq_in[t, d, e]
+        column = jnp.broadcast_to(total[0:1], (128, 128)).T[0:BW]
+        return lax.rsqrt(column * (1.0 / width) + 1e-06)
+
+    def scales(t):
+        for d, e in others:
+            landed(sq_in.at[t, d, e], q_s.at[t, d, e], q_r.at[t, d, e])
+        for e in range(m):
+            where = pl.ds(pl.multiple_of(blk_behind(e) * BW, BW), BW)
+            sq_out[where, :] = scale_of(t, e)
+        return sq_out[:, 0:1]
+
+    def combine(c_rows, weights):
+        lane = lax.broadcasted_iota(jnp.int32, (BW, count), 1)
+        line = lax.broadcasted_iota(jnp.int32, (BW, count), 0) + b * BW
+        diag = jnp.sum(jnp.where(lane == line, c_rows, 0.0), axis=1, keepdims=True)
+        off = jnp.where(lane == line, 0.0, c_rows)
+        moved = diag * v32[...] + nn(off.astype(BF16), low[...])
+        for j in range(n):
+            moved = moved + nn(weights(j).astype(BF16), feat[j])
+        return moved
+
+    kept = scatter(0, low[own, :], True)
+    gather(0, kept)
+    u32[...] = to_features(0)
+    kept = scatter(1, u32[...].astype(BF16), False)
+    gather(1, kept)
+    second = to_features(1).astype(BF16)
+    kept = scatter(2, second, False)
+
+    rest_landed(0)
+    for e in range(1, m):
+        peer = pl.ds(pl.multiple_of(blk_behind(e) * BW, BW), BW)
+        landed(low.at[peer], v_s.at[e], v_r.at[e])
+    cross = jnp.zeros((count, count), F32)
+    for j in range(n):
+        cross = cross + nt(chain[0, j], chain[0, j])
+    penalised(0, cross)
+    moved = v32[...] + u32[...] - nn(half[0, own, :].astype(BF16), low[...])
+    send_squares(0, moved, True)
+    gather(2, kept)
+
+    rest_landed(1)
+    d0 = scales(0)
+    h0 = half[0].astype(BF16)
+    cross = jnp.zeros((count, count), F32)
+    for j in range(n):
+        k0 = chain[0, j]
+        p1 = d0 * (k0.astype(F32) - nn(h0, k0) + chain[1, j].astype(F32))
+        proj[j] = p1
+        cross = cross + nt(p1.astype(BF16), p1.astype(BF16))
+    penalised(1, cross)
+    h1 = half[1].astype(BF16)
+    eye = jnp.where(
+        lax.broadcasted_iota(jnp.int32, (count, count), 0)
+        == lax.broadcasted_iota(jnp.int32, (count, count), 1), 1.0, 0.0,
+    )
+    c1 = d0 * (eye - half[0])
+    coef[...] = c1 - nn(h1, c1.astype(BF16))
+    for j in range(n):
+        w1 = d0 * chain[0, j].astype(F32) * (0.5 / total_tokens)
+        wsum[j] = w1 - nn(h1, w1.astype(BF16)) + proj[j] * (0.5 / total_tokens)
+    moved = combine(coef[own, :], lambda j: wsum[j, own, :])
+    send_squares(1, moved, True)
+
+    for d in range(1, n):
+        chain_landed(2, d, 0)
+    rest_landed(2)
+    for j in range(n):
+        k1 = chain[1, j]
+        q1 = d0 * (k1.astype(F32) - nn(h0, k1) + chain[2, j].astype(F32))
+        p1 = proj[j]
+        proj[j] = p1 - nn(h1, p1.astype(BF16)) + q1
+    d1 = scales(1)
+    cross = jnp.zeros((count, count), F32)
+    for j in range(n):
+        p2 = d1 * proj[j]
+        proj[j] = p2
+        wsum[j] = d1 * wsum[j]
+        cross = cross + nt(p2.astype(BF16), p2.astype(BF16))
+    penalised(2, cross)
+    coef[...] = d1 * coef[...]
+    h2 = half[2, own, :].astype(BF16)
+    c3 = coef[own, :] - nn(h2, coef[...].astype(BF16))
+
+    def last_weights(j):
+        return (
+            wsum[j, own, :] - nn(h2, wsum[j].astype(BF16)) + proj[j, own, :] * (0.5 / total_tokens)
+        )
+
+    moved = combine(c3, last_weights)
+    send_squares(2, moved, False)
+    v32[...] = moved
+    for d in range(1, n):
+        landed(sq_in.at[2, d, 0], q_s.at[2, d, 0], q_r.at[2, d, 0])
+    out_ref[...] = (v32[...] * scale_of(2, 0)[:, 0:1]).T
+    for copy in sent:
+        copy.wait_send()
+
+
+def fused_body(n, m, activations, directions, block_rank):
+    tokens = activations.shape[0]
+    rows = directions.shape[0]
+    count = m * BW
+    dma = pltpu.SemaphoreType.DMA
+    return pl.pallas_call(
+        functools.partial(fused, n, m),
+        out_shape=jax.ShapeDtypeStruct((rows, BW), F32),
+        in_specs=[
+            pl.BlockSpec(memory_space=pltpu.SMEM),
+            pl.BlockSpec(memory_space=pl.ANY),
+            pl.BlockSpec(memory_space=pltpu.VMEM),
+        ],
+        out_specs=pl.BlockSpec(memory_space=pltpu.VMEM),
+        scratch_shapes=[
+            pltpu.VMEM((n, tokens, rows), BF16),
+            pltpu.VMEM((count, rows), BF16),
+            pltpu.VMEM((BW, rows), F32),
+            pltpu.VMEM((BW, rows), F32),
+            pltpu.VMEM((ITERS, n, count, tokens), BF16),
+            pltpu.VMEM((ITERS, n, BW, tokens), F32),
+            pltpu.VMEM((ITERS, n, BW, tokens), F32),
+            pltpu.VMEM((n, count, tokens), F32),
+            pltpu.VMEM((n, count, tokens), F32),
+            pltpu.VMEM((ITERS, count, count), F32),
+            pltpu.VMEM((count, count), F32),
+            pltpu.VMEM((count, 128), F32),
+            pltpu.VMEM((ITERS, n, m, 8, 128), F32),
+            dma,
+            dma((n,)), dma((n,)),
+            dma((m,)), dma((m,)),
+            dma((ITERS, n)), dma((ITERS, n)),
+            dma((ITERS, n, m)), dma((ITERS, n, m)),
+            dma((ITERS, n, m)), dma((ITERS, n, m)),
+        ],
+        compiler_params=pltpu.CompilerParams(
+            collective_id=0, has_side_effects=True, vmem_limit_bytes=48 * 1024 * 1024
+        ),
+    )(block_rank, activations, directions)
+
+
 def solution(mesh):
+    n, m = mesh.shape["tok"], mesh.shape["blk"]
     placed = (P(("groups", "tok"), None), P(("groups", "tok"), "blk"), P())
+
+    def chosen(activations, directions, block_rank):
+        held = n * m * BW * activations.shape[0] * (3 * 2 + 2 * 4)
+        if held <= 16 * 1024 * 1024:
+            return fused_body(n, m, activations, directions, block_rank)
+        return body(activations, directions, block_rank)
+
     return jax.shard_map(
-        body, mesh=mesh, in_specs=placed, out_specs=P(("groups", "tok"), "blk"), check_vma=False
+        chosen, mesh=mesh, in_specs=placed, out_specs=P(("groups", "tok"), "blk"), check_vma=False
     )

time: 277 us -> 96.9 us (0.35)
  blocking collectives: 191 us -> 0 us
  Pallas kernels: 0 us -> 91.9 us
  waiting for transfers between devices: 28.6 us -> 0 us
  matrix products: 23.2 us -> 0 us
  between operations: 13.3 us -> 0.03 us
  other arithmetic: 7.08 us -> 0 us
  starting transfers between devices: 5.02 us -> 0 us
  local copies, waits for them, and re-layouts: 7.94 us -> 4.8 us
    all_gather x12 -> x0, blocking collectives: 173 us -> none  [the longest x3 57.8 us: body(): lax.all_gather(low, 'tok', axis=0, tiled=True)]
    pallas_call x0 -> x1, Pallas kernels: none -> 91.9 us  [fused_body(): pl.pallas_call(functools.partial(fused, n, m), out_shape=jax.ShapeDtypeSt...]
    psum x3 -> x0, waiting for transfers between devices: 28.5 us -> none  [body(): cross_row = lax.psum(partial_rows, 'tok') / (total_tokens * width)]
    dot_general x15 -> x0, matrix products: 23.2 us -> none  [the longest x3 7 us: body(): jnp.dot(activations, lax.all_gather(low, 'tok', axis=0, tiled=True), pref...]
    psum x3 -> x0, blocking collectives: 17.4 us -> none  [body(): squares = lax.psum(jnp.sum(moved * moved, axis=0), 'tok')]
    convert_element_type x6 -> x0, other arithmetic: 6 us -> none  [the longest x3 3.21 us: body(): low = current.astype(jnp.bfloat16)]
    all_to_all x1 -> x0, starting transfers between devices: 4.9 us -> none  [body(): lax.all_to_all(activations, 'tok', split_axis=1, concat_axis=0, tiled=True)]
    all_to_all x1 -> x0, local copies, waits for them, and re-layouts: 3.23 us -> none  [body(): lax.all_to_all(activations, 'tok', split_axis=1, concat_axis=0, tiled=True)]
  transfers between devices with their start and end apart: 4 -> 0, of which waited for: 3 -> 0; matrix products, arithmetic and copies ran while one was open for 3% -> 0% of each run, Pallas kernels for 0% -> 0%
where the time goes in v1:
time: 96.9 us; the launch traced here: 96.7 us
  Pallas kernels  91.9 us (95%)
  local copies, waits for them, and re-layouts  4.8 us (5%)
    pallas_call x1, Pallas kernels, fused_body(): pl.pallas_call(functools.partial(fused, n, m), out_shape=jax.ShapeDtypeSt...  91.9 us
    unnamed x5, local copies, waits for them, and re-layouts  3.8 us

profile of v1, /device:TPU:0, one launch (start us, length us, event | category | flops | bytes accessed | tf_op | source)
XLA Modules:
  0.0 96.7 jit_solution(502423315147445082)
XLA Ops:
  0.0 1.3 %copy.4.dir_ref = f32[1536,64]{1,0:T(8,128)S(1)} copy(f32[1536,64]{0,1:T(8,128)} %param.4) | data formatting | bytes 786432 | tf_op args[1]
  1.3 0.0 copy-start
  1.3 1.9 %copy-done = bf16[256,6144]{1,0:T(8,128)(2,1)S(1)} copy-done((bf16[256,6144]{1,0:T(8,128)(2,1)S(1)}, bf16[256,6144]{1,0:T(8,128)(2,1)}, u32[]{:S(2)}) %copy-start) | copy-done | bytes 3145752
  3.2 0.0 copy-start.1
  3.2 0.7 copy-done.1
  3.8 91.9 %shard_map.37 = f32[1536,64]{1,0:T(8,128)S(1)} custom-call(s32[4]{0:T(128)S(1)} %copy-done.1, bf16[256,6144]{1,0:T(8,128)(2,1)S(1)} %copy-done, f32[1536,64]{1,0:T(8,128)S(1)} %copy.4.dir_ref), custom_call_target="tpu_custom_call" | custom-call | tf_op jit(solution)/shard_map/pallas_call | solution.py:325
  95.7 1.0 %copy.5 = f32[1536,64]{0,1:T(8,128)} copy(f32[1536,64]{1,0:T(8,128)S(1)} %shard_map.37) | data formatting | bytes 786432 | tf_op jit(solution)/shard_map/pallas_call | solution.py:325
Async XLA Ops:
  1.3 1.9 %copy-start = (bf16[256,6144]{1,0:T(8,128)(2,1)S(1)}, bf16[256,6144]{1,0:T(8,128)(2,1)}, u32[]{:S(2)}) copy-start(bf16[256,6144]{1,0:T(8,128)(2,1)} %act_ref.1) | copy-start | bytes 9437188
  3.2 0.7 copy-start.1

commit v2 on v1

--- a/solution.py
+++ b/solution.py
@@ -106,7 +106,7 @@
 def fused(
     n, m, rank_ref, act_ref, dir_ref, out_ref,
     feat, low, v32, u32, chain, part, arrived, proj, wsum, half, coef, sq_out, sq_in,
-    f_loc, f_s, f_r, v_s, v_r, p_s, p_r, k_s, k_r, q_s, q_r,
+    f_loc, f_s, f_r, g_s, g_r, z_s, z_r, v_s, v_r, p_s, p_r, k_s, k_r, q_s, q_r,
 ):
     i, b = lax.axis_index("tok"), lax.axis_index("blk")
     tokens, rows = feat.shape[1], feat.shape[2]
@@ -114,11 +114,13 @@
     total_tokens, width = n * tokens, n * rows
     own = pl.ds(pl.multiple_of(b * BW, BW), BW)
 
+    chips = n // 2
+
     def ahead(d):
-        return lax.rem(i + d, n)
+        return lax.rem(i // 2 + d // 2, chips) * 2 + lax.rem(i + d, 2)
 
     def behind(d):
-        return lax.rem(i + n - d, n)
+        return lax.rem(i // 2 + chips - d // 2, chips) * 2 + lax.rem(i + d, 2)
 
     def blk_ahead(d):
         return lax.rem(b + d, m)
@@ -139,7 +141,7 @@
 
     def push(src, dst, s, r, d, e):
         copy = pltpu.make_async_remote_copy(
-            src_ref=src, dst_ref=dst, send_sem=s, recv_sem=r,
+            src_ref=src, dst_ref=dst, send_sem=s[0].at[s[1:]], recv_sem=r[0].at[r[1:]],
             device_id={"tok": ahead(d), "blk": blk_ahead(e)}, device_id_type=MESH,
         )
         copy.start()
@@ -147,46 +149,83 @@
 
     def landed(dst, s, r):
         pltpu.make_async_remote_copy(
-            src_ref=dst, dst_ref=dst, send_sem=s, recv_sem=r,
+            src_ref=dst, dst_ref=dst, send_sem=s[0].at[s[1:]], recv_sem=r[0].at[r[1:]],
             device_id={"tok": ahead(1)}, device_id_type=MESH,
         ).wait_recv()
 
-    for d in range(1, n):
-        cols = pl.ds(pl.multiple_of(ahead(d) * rows, 128), rows)
-        push(act_ref.at[:, cols], feat.at[i], f_s.at[d], f_r.at[d], d, 0)
+    direct = tokens // 2
+    share = (tokens - direct) // m
+    piece = pl.ds(pl.multiple_of(direct + b * share, share), share)
+
+    def columns_of(d):
+        return pl.ds(pl.multiple_of(ahead(d) * rows, 128), rows)
+
+    for d in range(2, n):
+        push(act_ref.at[piece, columns_of(d)], feat.at[i, piece], (g_s, d), (g_r, d), d, 0)
+    for d in range(2, n):
+        cols, top = columns_of(d), pl.ds(0, direct)
+        push(act_ref.at[top, cols], feat.at[i, top], (f_s, d), (f_r, d), d, 0)
+    push(act_ref.at[:, columns_of(1)], feat.at[i], (f_s, 1), (f_r, 1), 1, 0)
     mine = pltpu.make_async_copy(
         act_ref.at[:, pl.ds(pl.multiple_of(i * rows, 128), rows)], feat.at[i], f_loc
     )
     mine.start()
-    v32[...] = dir_ref[...].T
+    v32[...] = dir_ref[...]
     low[own, :] = v32[...].astype(BF16)
+    for d in range(2, n):
+        here = feat.at[behind(d), piece]
+        landed(here, (g_s, d), (g_r, d))
+        for e in range(1, m):
+            push(here, here, (z_s, d, e), (z_r, d, e), 0, e)
     for e in range(1, m):
-        push(low.at[own], low.at[own], v_s.at[e], v_r.at[e], 0, e)
+        push(low.at[own], low.at[own], (v_s, e), (v_r, e), 0, e)
+
+    def block_landed(d):
+        j = behind(d)
+        if d == 1:
+            landed(feat.at[j], (f_s, d), (f_r, d))
+            return
+        landed(feat.at[j, pl.ds(0, direct)], (f_s, d), (f_r, d))
+        for e in range(1, m):
+            other = pl.ds(pl.multiple_of(direct + blk_behind(e) * share, share), share)
+            landed(feat.at[j, other], (z_s, d, e), (z_r, d, e))
+
     mask = order_mask(rank_ref, m, count)
     mine.wait()
 
     def scatter(k, left, first):
         kept = nt(left, feat[i])
         for d in range(1, n):
+            back = ((chips - d // 2) % chips) * 2 + d % 2
             j = ahead(d)
             if first:
-                landed(feat.at[behind(n - d)], f_s.at[n - d], f_r.at[n - d])
+                block_landed(back)
             part[k, d] = nt(left, feat[j])
-            push(part.at[k, d], arrived.at[k, d], p_s.at[k, d], p_r.at[k, d], d, 0)
+            push(part.at[k, d], arrived.at[k, d], (p_s, k, d), (p_r, k, d), d, 0)
         return kept
 
     def gather(k, kept):
         for d in range(1, n):
-            landed(arrived.at[k, d], p_s.at[k, d], p_r.at[k, d])
+            landed(arrived.at[k, d], (p_s, k, d), (p_r, k, d))
             kept = kept + arrived[k, d]
         chain[k, i, own, :] = kept.astype(BF16)
-        for d, e in others:
-            tile = chain.at[k, i, own]
-            push(tile, tile, k_s.at[k, d, e], k_r.at[k, d, e], d, e)
+        tile = chain.at[k, i, own]
+        for d in range(1, n):
+            push(tile, tile, (k_s, k, d, 0), (k_r, k, d, 0), d, 0)
+        for e in range(1, m):
+            push(tile, tile, (k_s, k, 0, e), (k_r, k, 0, e), 0, e)
+
+    def pass_on(k):
+        for e in range(1, m):
+            chain_landed(k, 0, e)
+            peer = pl.ds(pl.multiple_of(blk_behind(e) * BW, BW), BW)
+            tile = chain.at[k, i, peer]
+            for d in range(1, n):
+                push(tile, tile, (k_s, k, d, e), (k_r, k, d, e), d, 0)
 
     def chain_landed(k, d, e):
         peer = pl.ds(pl.multiple_of(blk_behind(e) * BW, BW), BW)
-        landed(chain.at[k, behind(d), peer], k_s.at[k, d, e], k_r.at[k, d, e])
+        landed(chain.at[k, behind(d), peer], (k_s, k, d, e), (k_r, k, d, e))
 
     def to_features(k):
         total = nn(chain[k, i, own, :], feat[i])
@@ -198,7 +237,7 @@
 
     def rest_landed(k):
         for e in range(1, m):
-            for d in range(n):
+            for d in range(1, n):
                 chain_landed(k, d, e)
 
     def penalised(t, cross):
@@ -212,7 +251,7 @@
         sq_in[t, 0, 0] = block.T[0:8]
         for d, e in others:
             if everyone or e == 0:
-                push(sq_in.at[t, 0, 0], sq_in.at[t, d, e], q_s.at[t, d, e], q_r.at[t, d, e], d, e)
+                push(sq_in.at[t, 0, 0], sq_in.at[t, d, e], (q_s, t, d, e), (q_r, t, d, e), d, e)
 
     def scale_of(t, e):
         total = sq_in[t, 0, e]
@@ -223,7 +262,7 @@
 
     def scales(t):
         for d, e in others:
-            landed(sq_in.at[t, d, e], q_s.at[t, d, e], q_r.at[t, d, e])
+            landed(sq_in.at[t, d, e], (q_s, t, d, e), (q_r, t, d, e))
         for e in range(m):
             where = pl.ds(pl.multiple_of(blk_behind(e) * BW, BW), BW)
             sq_out[where, :] = scale_of(t, e)
@@ -243,14 +282,16 @@
     gather(0, kept)
     u32[...] = to_features(0)
     kept = scatter(1, u32[...].astype(BF16), False)
+    pass_on(0)
     gather(1, kept)
     second = to_features(1).astype(BF16)
     kept = scatter(2, second, False)
+    pass_on(1)
 
     rest_landed(0)
     for e in range(1, m):
         peer = pl.ds(pl.multiple_of(blk_behind(e) * BW, BW), BW)
-        landed(low.at[peer], v_s.at[e], v_r.at[e])
+        landed(low.at[peer], (v_s, e), (v_r, e))
     cross = jnp.zeros((count, count), F32)
     for j in range(n):
         cross = cross + nt(chain[0, j], chain[0, j])
@@ -258,6 +299,7 @@
     moved = v32[...] + u32[...] - nn(half[0, own, :].astype(BF16), low[...])
     send_squares(0, moved, True)
     gather(2, kept)
+    pass_on(2)
 
     rest_landed(1)
     d0 = scales(0)
@@ -311,8 +353,8 @@
     send_squares(2, moved, False)
     v32[...] = moved
     for d in range(1, n):
-        landed(sq_in.at[2, d, 0], q_s.at[2, d, 0], q_r.at[2, d, 0])
-    out_ref[...] = (v32[...] * scale_of(2, 0)[:, 0:1]).T
+        landed(sq_in.at[2, d, 0], (q_s, 2, d, 0), (q_r, 2, d, 0))
+    out_ref[...] = v32[...] * scale_of(2, 0)[:, 0:1]
     for copy in sent:
         copy.wait_send()
 
@@ -324,7 +366,7 @@
     dma = pltpu.SemaphoreType.DMA
     return pl.pallas_call(
         functools.partial(fused, n, m),
-        out_shape=jax.ShapeDtypeStruct((rows, BW), F32),
+        out_shape=jax.ShapeDtypeStruct((BW, rows), F32),
         in_specs=[
             pl.BlockSpec(memory_space=pltpu.SMEM),
             pl.BlockSpec(memory_space=pl.ANY),
@@ -347,15 +389,17 @@
             pltpu.VMEM((ITERS, n, m, 8, 128), F32),
             dma,
             dma((n,)), dma((n,)),
+            dma((n,)), dma((n,)),
+            dma((n, m)), dma((n, m)),
             dma((m,)), dma((m,)),
             dma((ITERS, n)), dma((ITERS, n)),
             dma((ITERS, n, m)), dma((ITERS, n, m)),
             dma((ITERS, n, m)), dma((ITERS, n, m)),
         ],
         compiler_params=pltpu.CompilerParams(
-            collective_id=0, has_side_effects=True, vmem_limit_bytes=48 * 1024 * 1024
+            collective_id=0, has_side_effects=True, vmem_limit_bytes=58 * 1024 * 1024
         ),
-    )(block_rank, activations, directions)
+    )(block_rank, activations, directions.T).T
 
 
 def solution(mesh):

time: 96.9 us -> 84.7 us (0.87)
  Pallas kernels: 91.9 us -> 82.8 us
  local copies, waits for them, and re-layouts: 4.8 us -> 1.77 us
    pallas_call x1, Pallas kernels: 91.9 us -> 82.8 us  [fused_body(): pl.pallas_call(functools.partial(fused, n, m), out_shape=jax.ShapeDtypeSt...]
    unnamed x5 -> x1, local copies, waits for them, and re-layouts: 3.8 us -> 1.77 us
    pallas_call x1 -> x0, local copies, waits for them, and re-layouts: 1 us -> none  [fused_body(): pl.pallas_call(functools.partial(fused, n, m), out_shape=jax.ShapeDtypeSt...]
where the time goes in v2:
time: 84.7 us; the launch traced here: 84.6 us
  Pallas kernels  82.8 us (98%)
  local copies, waits for them, and re-layouts  1.77 us (2%)
    pallas_call x1, Pallas kernels, fused_body(): pl.pallas_call(functools.partial(fused, n, m), out_shape=jax.ShapeDtypeSt...  82.8 us
    unnamed x1, local copies, waits for them, and re-layouts  1.77 us

profile of v2, /device:TPU:0, one launch (start us, length us, event | category | flops | bytes accessed | tf_op | source)
XLA Modules:
  0.0 84.6 jit_solution(13283138745491368363)
XLA Ops:
  0.0 82.8 %shard_map.37 = f32[64,1536]{1,0:T(8,128)} custom-call(s32[4]{0:T(128)} %rank_ref.1, bf16[256,6144]{1,0:T(8,128)(2,1)} %act_ref.1, f32[64,1536]{1,0:T(8,128)} %bitcast.3), custom_call_target="tpu_custom_call" | custom-call | tf_op jit(solution)/shard_map/pallas_call | solution.py:367
  82.8 1.8 %copy.5 = f32[1536,64]{0,1:T(8,128)} copy(f32[1536,64]{0,1:T(8,128)} %bitcast.2) | data formatting | bytes 786432

commit v3 on v2

--- a/solution.py
+++ b/solution.py
@@ -153,7 +153,7 @@
             device_id={"tok": ahead(1)}, device_id_type=MESH,
         ).wait_recv()
 
-    direct = tokens // 2
+    direct = tokens * 3 // 4
     share = (tokens - direct) // m
     piece = pl.ds(pl.multiple_of(direct + b * share, share), share)
 
@@ -172,13 +172,13 @@
     mine.start()
     v32[...] = dir_ref[...]
     low[own, :] = v32[...].astype(BF16)
+    for e in range(1, m):
+        push(low.at[own], low.at[own], (v_s, e), (v_r, e), 0, e)
     for d in range(2, n):
         here = feat.at[behind(d), piece]
         landed(here, (g_s, d), (g_r, d))
         for e in range(1, m):
             push(here, here, (z_s, d, e), (z_r, d, e), 0, e)
-    for e in range(1, m):
-        push(low.at[own], low.at[own], (v_s, e), (v_r, e), 0, e)
 
     def block_landed(d):
         j = behind(d)
@@ -282,10 +282,11 @@
     gather(0, kept)
     u32[...] = to_features(0)
     kept = scatter(1, u32[...].astype(BF16), False)
-    pass_on(0)
     gather(1, kept)
     second = to_features(1).astype(BF16)
     kept = scatter(2, second, False)
+    pass_on(0)
+    gather(2, kept)
     pass_on(1)
 
     rest_landed(0)
@@ -298,7 +299,6 @@
     penalised(0, cross)
     moved = v32[...] + u32[...] - nn(half[0, own, :].astype(BF16), low[...])
     send_squares(0, moved, True)
-    gather(2, kept)
     pass_on(2)
 
     rest_landed(1)
@@ -408,7 +408,7 @@
 
     def chosen(activations, directions, block_rank):
         held = n * m * BW * activations.shape[0] * (3 * 2 + 2 * 4)
-        if held <= 16 * 1024 * 1024:
+        if held <= 16 * 1024 * 1024 and activations.shape[0] % (64 * m) == 0:
             return fused_body(n, m, activations, directions, block_rank)
         return body(activations, directions, block_rank)
 

time: 84.7 us -> 85 us (level)
  no operation moved by 1% of the time
where the time goes in v3:
time: 85 us; the launch traced here: 84.8 us
  Pallas kernels  83.1 us (98%)
  local copies, waits for them, and re-layouts  1.77 us (2%)
    pallas_call x1, Pallas kernels, fused_body(): pl.pallas_call(functools.partial(fused, n, m), out_shape=jax.ShapeDtypeSt...  83.1 us
    unnamed x1, local copies, waits for them, and re-layouts  1.77 us

profile of v3, /device:TPU:0, one launch (start us, length us, event | category | flops | bytes accessed | tf_op | source)
XLA Modules:
  0.0 84.8 jit_solution(4090000268681147840)
XLA Ops:
  0.0 83.1 %shard_map.37 = f32[64,1536]{1,0:T(8,128)} custom-call(s32[4]{0:T(128)} %rank_ref.1, bf16[256,6144]{1,0:T(8,128)(2,1)} %act_ref.1, f32[64,1536]{1,0:T(8,128)} %bitcast.3), custom_call_target="tpu_custom_call" | custom-call | tf_op jit(solution)/shard_map/pallas_call | solution.py:367
  83.1 1.8 %copy.5 = f32[1536,64]{0,1:T(8,128)} copy(f32[1536,64]{0,1:T(8,128)} %bitcast.2) | data formatting | bytes 786432

commit v4 on v3

--- a/solution.py
+++ b/solution.py
@@ -200,14 +200,14 @@
             j = ahead(d)
             if first:
                 block_landed(back)
-            part[k, d] = nt(left, feat[j])
+            part[k, d] = nt(left, feat[j]).astype(BF16)
             push(part.at[k, d], arrived.at[k, d], (p_s, k, d), (p_r, k, d), d, 0)
         return kept
 
     def gather(k, kept):
         for d in range(1, n):
             landed(arrived.at[k, d], (p_s, k, d), (p_r, k, d))
-            kept = kept + arrived[k, d]
+            kept = kept + arrived[k, d].astype(F32)
         chain[k, i, own, :] = kept.astype(BF16)
         tile = chain.at[k, i, own]
         for d in range(1, n):
@@ -379,8 +379,8 @@
             pltpu.VMEM((BW, rows), F32),
             pltpu.VMEM((BW, rows), F32),
             pltpu.VMEM((ITERS, n, count, tokens), BF16),
-            pltpu.VMEM((ITERS, n, BW, tokens), F32),
-            pltpu.VMEM((ITERS, n, BW, tokens), F32),
+            pltpu.VMEM((ITERS, n, BW, tokens), BF16),
+            pltpu.VMEM((ITERS, n, BW, tokens), BF16),
             pltpu.VMEM((n, count, tokens), F32),
             pltpu.VMEM((n, count, tokens), F32),
             pltpu.VMEM((ITERS, count, count), F32),

time: 85 us -> 81.7 us (0.961)
  Pallas kernels: 83.1 us -> 79.7 us
    pallas_call x1, Pallas kernels: 83.1 us -> 79.7 us  [fused_body(): pl.pallas_call(functools.partial(fused, n, m), out_shape=jax.ShapeDtypeSt...]
where the time goes in v4:
time: 81.7 us; the launch traced here: 81.5 us
  Pallas kernels  79.7 us (98%)
  local copies, waits for them, and re-layouts  1.77 us (2%)
    pallas_call x1, Pallas kernels, fused_body(): pl.pallas_call(functools.partial(fused, n, m), out_shape=jax.ShapeDtypeSt...  79.7 us
    unnamed x1, local copies, waits for them, and re-layouts  1.77 us

profile of v4, /device:TPU:0, one launch (start us, length us, event | category | flops | bytes accessed | tf_op | source)
XLA Modules:
  0.0 81.5 jit_solution(783689417192774106)
XLA Ops:
  0.0 79.7 %shard_map.37 = f32[64,1536]{1,0:T(8,128)} custom-call(s32[4]{0:T(128)} %rank_ref.1, bf16[256,6144]{1,0:T(8,128)(2,1)} %act_ref.1, f32[64,1536]{1,0:T(8,128)} %bitcast.3), custom_call_target="tpu_custom_call" | custom-call | tf_op jit(solution)/shard_map/pallas_call | solution.py:367
  79.8 1.8 %copy.5 = f32[1536,64]{0,1:T(8,128)} copy(f32[1536,64]{0,1:T(8,128)} %bitcast.2) | data formatting | bytes 786432
